TPU v7x, 32 devices: a whole 2x2x4 slice. The times are simulated.
32 devices in a mesh: fsdp: 8 (over z, core), mp: 4 (over y, x).
Axes of the slice: x: 2, y: 2, z: 4, core: 2. Of those that a mesh axis runs over, the one named last changes fastest.
Arguments:
- inputs: bfloat16 [2048, 2048], P('fsdp'), may hold values from -6 to 6
- cotangent: bfloat16 [2048, 2048], P('fsdp'), may hold values from -6 to 6
- lengths: int32 [2], replicated, may hold values from 256 to 1024, as said below
- attn_scale: float32 [2048], P('fsdp'), may hold values from 0.5 to 1.5
- w_query: float32 [2048, 2048], P('fsdp', 'mp'), may hold values from -0.015625 to 0.015625
- w_key: float32 [2048, 2048], P('fsdp', 'mp'), may hold values from -0.125 to 0.125
- w_value: float32 [2048, 2048], P('fsdp', 'mp'), may hold values from -0.125 to 0.125
- w_out: float32 [2048, 2048], P('mp', 'fsdp'), may hold values from -3 to 3
- rel_table: float32 [32, 32], P('fsdp', 'mp'), may hold values from -4 to 4
- ffn_scale: float32 [2048], P('fsdp'), may hold values from 0.5 to 1.5
- w_gate: float32 [2048, 5120], P('fsdp', 'mp'), may hold values from -0.125 to 0.125
- w_up: float32 [2048, 5120], P('fsdp', 'mp'), may hold values from -0.125 to 0.125
- w_down: float32 [5120, 2048], P('mp', 'fsdp'), may hold values from -0.078125 to 0.078125
Outputs:
- outputs: bfloat16 [2048, 2048], P('fsdp')
- d_inputs: bfloat16 [2048, 2048], P('fsdp')
- d_attn_scale: float32 [2048], P('fsdp')
- d_w_query: float32 [2048, 2048], P('fsdp', 'mp')
- d_w_key: float32 [2048, 2048], P('fsdp', 'mp')
- d_w_value: float32 [2048, 2048], P('fsdp', 'mp')
- d_w_out: float32 [2048, 2048], P('mp', 'fsdp')
- d_rel_table: float32 [32, 32], P('fsdp', 'mp')
- d_ffn_scale: float32 [2048], P('fsdp')
- d_w_gate: float32 [2048, 5120], P('fsdp', 'mp')
- d_w_up: float32 [2048, 5120], P('fsdp', 'mp')
- d_w_down: float32 [5120, 2048], P('mp', 'fsdp')
Inputs may be any that keep to these rules, and one draw needn't show every extreme that they name: lengths[s] slots at the start of sequence s are used, the rest is padding; in every draw some sequence is full.
All inputs are finite; a program needn't handle non-finite values.
Results may differ from a plain program's by a relative error of at most 0.019.
Values may be sent and summed in bfloat16 or wider, within the bound.
No kernel may reach another device: no remote copies, remote signals or barrier semaphores. Data moves between devices by JAX's collectives and lax.ppermute only.
A program may use at most 192 MiB of HBM per device.

v0:
```python
import jax
import jax.numpy as jnp
from jax import lax
from jax.sharding import PartitionSpec as P

GROUP = 4
THRESHOLDS = (12, 16, 23, 32, 46, 64, 91)
EPSILON = 1e-06
MASKED = -1e30


def shifted(block, axis, distance):
    devices = range(lax.axis_size(axis))
    route = [(i - distance, i) for i in devices if i - distance in devices]
    return lax.ppermute(block, axis, route)


def bucket_of(rel_offset):
    distance = jnp.abs(rel_offset)
    far_bucket = 8 + sum(((distance >= threshold).astype(jnp.int32) for threshold in THRESHOLDS))
    bucket_abs = jnp.where(distance < 8, distance, far_bucket)
    return bucket_abs + jnp.where(rel_offset > 0, 16, 0)


def bucket_onehot(first_query, query_count, key_count, bucket_count):
    span_width = query_count + key_count
    rel_offset = lax.iota(jnp.int32, span_width) - (first_query + query_count - 1)
    return (bucket_of(rel_offset)[:, None] == lax.iota(jnp.int32, bucket_count)[None, :]).astype(
        jnp.float32
    )


def offset_bias(table_f32, first_query, query_count, key_count):
    span_width = query_count + key_count
    one_hot = bucket_onehot(first_query, query_count, key_count, table_f32.shape[0])
    bias_line = jnp.dot(one_hot, table_f32, precision=lax.Precision.HIGHEST).T
    repeated = jnp.tile(bias_line, (1, query_count))
    skewed = lax.slice_in_dim(
        repeated, query_count - 1, query_count - 1 + query_count * (span_width - 1), axis=1
    )
    return skewed.reshape(bias_line.shape[0], query_count, span_width - 1)[:, :, :key_count]


def offset_grad(grad_scores, first_query, query_count, key_count, bucket_count):
    span_width = query_count + key_count
    head_count = grad_scores.shape[0]
    widened = jnp.pad(grad_scores, ((0, 0), (0, 0), (0, span_width - 1 - key_count)))
    flattened = jnp.pad(
        widened.reshape(head_count, query_count * (span_width - 1)), ((0, 0), (query_count - 1, 1))
    )
    summed = jnp.sum(flattened.reshape(head_count, query_count, span_width), axis=1)
    one_hot = bucket_onehot(first_query, query_count, key_count, bucket_count)
    return jnp.dot(one_hot.T, summed.T, precision=lax.Precision.HIGHEST)


def contract_rows(left, right):
    return lax.dot_general(
        left, right, (((0,), (0,)), ((), ())), preferred_element_type=jnp.float32
    )


def contract_cols(left, right):
    return lax.dot_general(
        left, right, (((1,), (1,)), ((), ())), preferred_element_type=jnp.float32
    )


def gelu_tanh(values):
    return jax.nn.gelu(values, approximate=True)


def group_collect(keys_local, values_local, member, tok_rows):
    key_pieces = []
    value_pieces = []
    for distance in range(GROUP - 1, -GROUP, -1):
        if distance == 0:
            key_pieces.append(keys_local)
            value_pieces.append(values_local)
        else:
            moved_keys, moved_values = shifted((keys_local, values_local), "fsdp", distance)
            key_pieces.append(moved_keys)
            value_pieces.append(moved_values)
    first_piece = GROUP - 1 - member
    keys_seq = lax.dynamic_slice_in_dim(jnp.stack(key_pieces), first_piece, GROUP, 0)
    values_seq = lax.dynamic_slice_in_dim(jnp.stack(value_pieces), first_piece, GROUP, 0)
    return (keys_seq.reshape(GROUP * tok_rows, -1), values_seq.reshape(GROUP * tok_rows, -1))


def group_return(keys_part, values_part, member, tok_rows):
    own_keys = lax.dynamic_slice_in_dim(keys_part, member * tok_rows, tok_rows, 0)
    own_values = lax.dynamic_slice_in_dim(values_part, member * tok_rows, tok_rows, 0)
    for distance in list(range(1, GROUP)) + list(range(-1, -GROUP, -1)):
        target = member + distance
        inside = (target >= 0) & (target < GROUP)
        clamped = jnp.clip(target, 0, GROUP - 1)
        send_keys = jnp.where(
            inside, lax.dynamic_slice_in_dim(keys_part, clamped * tok_rows, tok_rows, 0), 0.0
        )
        send_values = jnp.where(
            inside, lax.dynamic_slice_in_dim(values_part, clamped * tok_rows, tok_rows, 0), 0.0
        )
        got_keys, got_values = shifted((send_keys, send_values), "fsdp", distance)
        own_keys = own_keys + got_keys
        own_values = own_values + got_values
    return (own_keys, own_values)


def local(
    inputs,
    cotangent,
    lengths,
    attn_scale,
    w_query,
    w_key,
    w_value,
    w_out,
    rel_table,
    ffn_scale,
    w_gate,
    w_up,
    w_down,
):
    low_type = jnp.bfloat16
    tok_rows = inputs.shape[0]
    seq_len = tok_rows * GROUP
    block_rows = min(512, tok_rows)
    block_count = tok_rows // block_rows
    position = lax.axis_index("fsdp")
    member = position % GROUP
    sequence = position // GROUP
    length = lax.dynamic_index_in_dim(lengths, sequence, 0, keepdims=False)
    first_row = member * tok_rows
    query_valid = first_row + lax.iota(jnp.int32, tok_rows) < length
    key_valid = lax.iota(jnp.int32, seq_len) < length
    resid = inputs.astype(jnp.float32)
    gain_one, query_full, key_full, value_full, out_full, table_low = (
        lax.all_gather(attn_scale.astype(low_type), "fsdp", axis=0, tiled=True),
        lax.all_gather(w_query.astype(low_type), "fsdp", axis=0, tiled=True),
        lax.all_gather(w_key.astype(low_type), "fsdp", axis=0, tiled=True),
        lax.all_gather(w_value.astype(low_type), "fsdp", axis=0, tiled=True),
        lax.all_gather(w_out.astype(low_type), "fsdp", axis=1, tiled=True),
        lax.all_gather(rel_table.astype(low_type), "fsdp", axis=0, tiled=True),
    )
    gain_one = gain_one.astype(jnp.float32)
    table_f32 = table_low.astype(jnp.float32)
    bucket_count = table_f32.shape[0]
    head_count = table_f32.shape[1]
    inner_width = query_full.shape[1]
    head_width = inner_width // head_count
    inv_one = lax.rsqrt(jnp.mean(resid * resid, axis=1, keepdims=True) + EPSILON)
    normed_one = resid * inv_one
    hidden_one = (normed_one * gain_one).astype(low_type)
    queries = jnp.dot(hidden_one, query_full, preferred_element_type=jnp.float32).astype(low_type)
    keys_local = jnp.dot(hidden_one, key_full, preferred_element_type=jnp.float32).astype(low_type)
    values_local = jnp.dot(hidden_one, value_full, preferred_element_type=jnp.float32).astype(
        low_type
    )
    keys_seq, values_seq = group_collect(keys_local, values_local, member, tok_rows)
    query_heads = queries.reshape(tok_rows, head_count, head_width)
    key_heads = keys_seq.reshape(seq_len, head_count, head_width)
    value_heads = values_seq.reshape(seq_len, head_count, head_width)

    def scores_of(block_start):
        pos_bias = offset_bias(table_f32, first_row + block_start, block_rows, seq_len)
        raw_scores = (
            jnp.einsum("qhd,khd->hqk", query_heads, key_heads, preferred_element_type=jnp.float32)
            + pos_bias
        )
        return (query_heads, jnp.where(key_valid[None, None, :], raw_scores, MASKED))

    def forward_block(block_index):
        query_block, raw_scores = scores_of(block_index * block_rows)
        row_max = jnp.max(raw_scores, axis=2, keepdims=True)
        exp_scores = jnp.exp(raw_scores - row_max)
        row_total = jnp.sum(exp_scores, axis=2, keepdims=True)
        attn_prob = (exp_scores / row_total).astype(low_type)
        block_out = jnp.einsum(
            "hqk,khd->qhd", attn_prob, value_heads, preferred_element_type=jnp.float32
        ).astype(low_type)
        return (block_out, row_max[:, :, 0] + jnp.log(row_total[:, :, 0]))

    attended, log_total = lax.map(forward_block, lax.iota(jnp.int32, block_count))
    attended = attended.reshape(tok_rows, inner_width)
    gain_two, gate_full, up_full, down_full = (
        lax.all_gather(ffn_scale.astype(low_type), "fsdp", axis=0, tiled=True),
        lax.all_gather(w_gate.astype(low_type), "fsdp", axis=0, tiled=True),
        lax.all_gather(w_up.astype(low_type), "fsdp", axis=0, tiled=True),
        lax.all_gather(w_down.astype(low_type), "fsdp", axis=1, tiled=True),
    )
    gain_two = gain_two.astype(jnp.float32)
    mixed_attn = lax.psum(jnp.dot(attended, out_full, preferred_element_type=jnp.float32), "mp")
    after_attn = resid + mixed_attn
    inv_two = lax.rsqrt(jnp.mean(after_attn * after_attn, axis=1, keepdims=True) + EPSILON)
    normed_two = after_attn * inv_two
    hidden_rows = (normed_two * gain_two).astype(low_type)
    gate_pre = jnp.dot(hidden_rows, gate_full, preferred_element_type=jnp.float32)
    up_pre = jnp.dot(hidden_rows, up_full, preferred_element_type=jnp.float32)
    gelu_value, gelu_pull = jax.vjp(gelu_tanh, gate_pre)
    hidden_act = (gelu_value * up_pre).astype(low_type)
    mixed_ffn = lax.psum(
        jnp.dot(hidden_act, down_full, preferred_element_type=jnp.float32).astype(jnp.bfloat16),
        "mp",
    ).astype(jnp.float32)
    after_ffn = after_attn + mixed_ffn
    layer_out = jnp.where(query_valid[:, None], after_ffn, 0.0).astype(low_type)
    grad_two = jnp.where(query_valid[:, None], cotangent.astype(jnp.float32), 0.0)
    grad_two_low = grad_two.astype(low_type)
    d_down = contract_rows(hidden_act, grad_two_low)
    d_hidden = contract_cols(grad_two_low, down_full)
    (d_gate_pre,) = gelu_pull(d_hidden * up_pre)
    d_gate_low = d_gate_pre.astype(low_type)
    d_up_low = (d_hidden * gelu_value).astype(low_type)
    d_gate_w = contract_rows(hidden_rows, d_gate_low)
    d_up_w = contract_rows(hidden_rows, d_up_low)
    d_norm_two = lax.psum(
        contract_cols(d_gate_low, gate_full) + contract_cols(d_up_low, up_full), "mp"
    )
    d_gain_two = jnp.sum(d_norm_two * normed_two, axis=0)
    ffn_grads = (
        lax.psum_scatter(d_gain_two, "fsdp", scatter_dimension=0, tiled=True),
        lax.psum_scatter(d_gate_w, "fsdp", scatter_dimension=0, tiled=True),
        lax.psum_scatter(d_up_w, "fsdp", scatter_dimension=0, tiled=True),
        lax.psum_scatter(d_down, "fsdp", scatter_dimension=1, tiled=True),
    )
    inner_two = d_norm_two * gain_two
    grad_one = grad_two + inv_two * (
        inner_two - normed_two * jnp.mean(inner_two * normed_two, axis=1, keepdims=True)
    )
    grad_one_rows_low = grad_one.astype(low_type)
    d_out_w = contract_rows(attended, grad_one_rows_low)
    d_attended = contract_cols(grad_one_rows_low, out_full).astype(low_type)
    d_out_heads = d_attended.reshape(tok_rows, head_count, head_width)

    def backward_block(carry, block_index):
        d_keys, d_values, d_table = carry
        block_start = block_index * block_rows
        query_block, raw_scores = scores_of(block_start)
        block_lse = lax.dynamic_index_in_dim(log_total, block_index, 0, keepdims=False)
        attn_prob = jnp.exp(raw_scores - block_lse[:, :, None])
        d_prob = jnp.einsum(
            "qhd,khd->hqk", d_out_heads, value_heads, preferred_element_type=jnp.float32
        )
        d_scores = (
            attn_prob * (d_prob - jnp.sum(attn_prob * d_prob, axis=2, keepdims=True))
        ).astype(low_type)
        d_query_block = jnp.einsum(
            "hqk,khd->qhd", d_scores, key_heads, preferred_element_type=jnp.float32
        ).astype(low_type)
        d_keys = d_keys + jnp.einsum(
            "hqk,qhd->khd", d_scores, query_block, preferred_element_type=jnp.float32
        )
        d_values = d_values + jnp.einsum(
            "hqk,qhd->khd",
            attn_prob.astype(low_type),
            d_out_heads,
            preferred_element_type=jnp.float32,
        )
        d_table = d_table + offset_grad(
            d_scores.astype(jnp.float32), first_row + block_start, block_rows, seq_len, bucket_count
        )
        return ((d_keys, d_values, d_table), d_query_block)

    zero_keys = jnp.zeros((seq_len, head_count, head_width), jnp.float32)
    zero_table = jnp.zeros((bucket_count, head_count), jnp.float32)
    (d_keys_seq, d_values_seq, d_table), d_query_blocks = lax.scan(
        backward_block, (zero_keys, zero_keys, zero_table), lax.iota(jnp.int32, block_count)
    )
    d_queries_low = d_query_blocks.reshape(tok_rows, inner_width)
    d_keys_seq = d_keys_seq.reshape(seq_len, inner_width)
    d_values_seq = d_values_seq.reshape(seq_len, inner_width)
    mine_keys, mine_values = group_return(d_keys_seq, d_values_seq, member, tok_rows)
    d_keys_low = mine_keys.astype(low_type)
    d_values_low = mine_values.astype(low_type)
    d_query_w = contract_rows(hidden_one, d_queries_low)
    d_key_w = contract_rows(hidden_one, d_keys_low)
    d_value_w = contract_rows(hidden_one, d_values_low)
    norm_part = (
        contract_cols(d_queries_low, query_full)
        + contract_cols(d_keys_low, key_full)
        + contract_cols(d_values_low, value_full)
    )
    d_norm_one = lax.psum(norm_part, "mp")
    d_gain_one = jnp.sum(d_norm_one * normed_one, axis=0)
    attn_grads = (
        lax.psum_scatter(d_gain_one, "fsdp", scatter_dimension=0, tiled=True),
        lax.psum_scatter(d_query_w, "fsdp", scatter_dimension=0, tiled=True),
        lax.psum_scatter(d_key_w, "fsdp", scatter_dimension=0, tiled=True),
        lax.psum_scatter(d_value_w, "fsdp", scatter_dimension=0, tiled=True),
        lax.psum_scatter(d_out_w, "fsdp", scatter_dimension=1, tiled=True),
        lax.psum_scatter(d_table, "fsdp", scatter_dimension=0, tiled=True),
    )
    inner_one = d_norm_one * gain_one
    grad_input = grad_one + inv_one * (
        inner_one - normed_one * jnp.mean(inner_one * normed_one, axis=1, keepdims=True)
    )
    grad_input_low = grad_input.astype(low_type)
    return (
        layer_out,
        grad_input_low,
        attn_grads[0],
        attn_grads[1],
        attn_grads[2],
        attn_grads[3],
        attn_grads[4],
        attn_grads[5],
        ffn_grads[0],
        ffn_grads[1],
        ffn_grads[2],
        ffn_grads[3],
    )


def solution(mesh):
    in_specs = (
        P("fsdp", None),
        P("fsdp", None),
        P(),
        P("fsdp"),
        P("fsdp", "mp"),
        P("fsdp", "mp"),
        P("fsdp", "mp"),
        P("mp", "fsdp"),
        P("fsdp", "mp"),
        P("fsdp"),
        P("fsdp", "mp"),
        P("fsdp", "mp"),
        P("mp", "fsdp"),
    )
    out_specs = (
        P("fsdp", None),
        P("fsdp", None),
        P("fsdp"),
        P("fsdp", "mp"),
        P("fsdp", "mp"),
        P("fsdp", "mp"),
        P("mp", "fsdp"),
        P("fsdp", "mp"),
        P("fsdp"),
        P("fsdp", "mp"),
        P("fsdp", "mp"),
        P("mp", "fsdp"),
    )
    return jax.shard_map(local, mesh=mesh, in_specs=in_specs, out_specs=out_specs, check_vma=False)
```

profile of v0, /device:TPU:0, one launch (start us, length us, event | category | flops | bytes accessed | tf_op | source)
XLA Modules:
  0.0 1290.1 jit_solution(14534975958745252116)
XLA Ops:
  12.8 13.5 %all-gather = bf16[8,1,256]{2,1,0:T(2,128)(2,1)S(1)} all-gather(bf16[1,1,256]{2,1,0:T(2,128)(2,1)S(1)} %reshape.151), channel_id=1, replica_groups=mesh['fsdp'=8,'mp'=4] {'fsdp'}, dimensions={0}, use_global_device_ids=true | all-gather | bytes 4608 | tf_op jit(solution)/shard_map/all_gather | solution.py:137
  50.7 20.7 %reshape.140 = f32[8,256,1279]{2,1,0:T(8,128)} reshape(f32[2619392]{0:T(1024)} %reshape.162) | data formatting | bytes 20955136 | tf_op jit(solution)/shard_map/while/body/eval_jaxpr/reshape | solution.py:41
  88.2 23.7 %all-gather.13.cloned.1.call-done = bf16[2048,512]{1,0:T(8,128)(2,1)} async-done(((bf16[256,512]{1,0:T(8,128)(2,1)}), bf16[2048,512]{1,0:T(8,128)(2,1)}) %all-gather.13.cloned.1.call-update) | async-done | bytes 2097168 | tf_op jit(solution)/shard_map/all_gather | solution.py:138
  146.2 17.2 %collective-permute-done.4 = bf16[256,512]{1,0:T(8,128)(2,1)S(1)} collective-permute-done((bf16[256,512]{1,0:T(8,128)(2,1)S(1)}, bf16[256,512]{1,0:T(8,128)(2,1)S(1)}, u32[]{:S(2)}, u32[]{:S(2)}) %collective-permute-start.4) | collective-permute-done | bytes 262176 | tf_op jit(solution)/shard_map/ppermute | solution.py:15
  194.5 16.0 %all-gather.2 = bf16[8,1,256]{2,1,0:T(2,128)(2,1)S(1)} all-gather(bf16[1,1,256]{2,1,0:T(2,128)(2,1)S(1)} %reshape.155), channel_id=1, replica_groups=mesh['fsdp'=8,'mp'=4] {'fsdp'}, dimensions={0}, use_global_device_ids=true | all-gather | bytes 4608 | tf_op jit(solution)/shard_map/all_gather | solution.py:185
  211.1 52.6 %all-reduce.11.cloned.1.call-done = f32[256,2048]{1,0:T(8,128)} async-done(((f32[256,2048]{1,0:T(8,128)}), f32[256,2048]{1,0:T(8,128)}) %all-reduce.11.cloned.1.call-update) | async-done | bytes 2097168 | tf_op jit(solution)/shard_map/psum | solution.py:191
  267.1 54.9 %all-gather.19.cloned.1.call-done = bf16[2048,1280]{1,0:T(8,128)(2,1)} async-done(((bf16[256,1280]{1,0:T(8,128)(2,1)}), bf16[2048,1280]{1,0:T(8,128)(2,1)}) %all-gather.19.cloned.1.call-update) | async-done | bytes 5242896 | tf_op jit(solution)/shard_map/all_gather | solution.py:186
  327.3 51.8 %all-gather.21.cloned.1.call-done = bf16[2048,1280]{1,0:T(8,128)(2,1)} async-done(((bf16[256,1280]{1,0:T(8,128)(2,1)}), bf16[2048,1280]{1,0:T(8,128)(2,1)}) %all-gather.21.cloned.1.call-update) | async-done | bytes 5242896 | tf_op jit(solution)/shard_map/all_gather | solution.py:187
  384.5 51.6 %all-gather.23.cloned.1.call-done = bf16[1280,2048]{1,0:T(8,128)(2,1)} async-done(((bf16[1280,256]{1,0:T(8,128)(2,1)}), bf16[1280,2048]{1,0:T(8,128)(2,1)}) %all-gather.23.cloned.1.call-update) | async-done | bytes 5242896 | tf_op jit(solution)/shard_map/all_gather | solution.py:188
  454.5 62.4 %all-reduce.15.cloned.1.call-done = f32[256,2048]{1,0:T(8,128)} async-done(((f32[256,2048]{1,0:T(8,128)}), f32[256,2048]{1,0:T(8,128)}) %all-reduce.15.cloned.1.call-update) | async-done | bytes 2097168 | tf_op jit(solution)/shard_map/psum | solution.py:215
  519.1 53.9 %all-reduce.13.cloned.1.call-done = bf16[256,2048]{1,0:T(8,128)(2,1)} async-done(((bf16[256,2048]{1,0:T(8,128)(2,1)}), bf16[256,2048]{1,0:T(8,128)(2,1)}) %all-reduce.13.cloned.1.call-update) | async-done | bytes 1048592 | tf_op jit(solution)/shard_map/psum | solution.py:200
  622.4 14.0 %collective-permute-start.20 = (f32[256,512]{0,1:T(8,128)S(1)}, f32[256,512]{0,1:T(8,128)S(1)}, u32[]{:S(2)}, u32[]{:S(2)}) collective-permute-start(f32[256,512]{0,1:T(8,128)S(1)} %get-tuple-element.96), channel_id=1, source_target_pairs={{0,12},{4,16},{8,20},{12,24},{16,28},{1,13},{5,17},{9,21},{13,25},... | collective-permute-start | bytes 1572872 | tf_op jit(solution)/shard_map/ppermute | solution.py:15
  640.2 9.0 collective-permute-start.18
  705.5 11.6 reshape.164
  717.1 10.4 reshape.146
  733.5 11.1 all-reduce.17.cloned.1.call-done
  746.8 30.1 %all-reduce.5 = (f32[2048]{0:T(1024)S(1)}, f32[32,8]{1,0:T(8,128)S(1)}, f32[2048]{0:T(1024)S(1)}) all-reduce(f32[2048]{0:T(1024)S(1)} %get-tuple-element.67, f32[32,8]{1,0:T(8,128)S(1)} %fusion.36, f32[2048]{0:T(1024)S(1)} %get-tuple-element.65), channel_id=2, replica_groups=mesh['fsdp'=8,'mp'=4] {'fsdp'}, use_global_device_ids=true, to_apply=%region_12.13.clone | all-reduce | flops 4352 | bytes 34816
  781.9 16.0 %reduce-scatter.8.cloned.1.call-done = f32[256,512]{1,0:T(8,128)} async-done(((f32[2048,512]{1,0:T(8,128)}), f32[256,512]{1,0:T(8,128)}) %reduce-scatter.8.cloned.1.call-update) | async-done | bytes 524304 | tf_op jit(solution)/shard_map/reduce_scatter | solution.py:286
  797.9 51.1 %reduce-scatter.14.cloned.1.call-done = f32[512,256]{1,0:T(8,128)} async-done(((f32[512,2048]{1,0:T(8,128)}), f32[512,256]{1,0:T(8,128)}) %reduce-scatter.14.cloned.1.call-update) | async-done | bytes 524304 | tf_op jit(solution)/shard_map/reduce_scatter | solution.py:289
  849.1 51.0 %reduce-scatter.10.cloned.1.call-done = f32[256,512]{1,0:T(8,128)} async-done(((f32[2048,512]{1,0:T(8,128)}), f32[256,512]{1,0:T(8,128)}) %reduce-scatter.10.cloned.1.call-update) | async-done | bytes 524304 | tf_op jit(solution)/shard_map/reduce_scatter | solution.py:287
  900.1 51.0 %reduce-scatter.12.cloned.1.call-done = f32[256,512]{1,0:T(8,128)} async-done(((f32[2048,512]{1,0:T(8,128)}), f32[256,512]{1,0:T(8,128)}) %reduce-scatter.12.cloned.1.call-update) | async-done | bytes 524304 | tf_op jit(solution)/shard_map/reduce_scatter | solution.py:288
  951.1 110.4 %reduce-scatter.16.cloned.1.call-done = f32[256,1280]{1,0:T(8,128)} async-done(((f32[2048,1280]{1,0:T(8,128)}), f32[256,1280]{1,0:T(8,128)}) %reduce-scatter.16.cloned.1.call-update) | async-done | bytes 1310736 | tf_op jit(solution)/shard_map/reduce_scatter | solution.py:221
  1061.5 110.6 %reduce-scatter.18.cloned.1.call-done = f32[256,1280]{1,0:T(8,128)} async-done(((f32[2048,1280]{1,0:T(8,128)}), f32[256,1280]{1,0:T(8,128)}) %reduce-scatter.18.cloned.1.call-update) | async-done | bytes 1310736 | tf_op jit(solution)/shard_map/reduce_scatter | solution.py:222
  1172.2 110.6 %reduce-scatter.20.cloned.1.call-done = f32[1280,256]{1,0:T(8,128)} async-done(((f32[1280,2048]{1,0:T(8,128)}), f32[1280,256]{1,0:T(8,128)}) %reduce-scatter.20.cloned.1.call-update) | async-done | bytes 1310736 | tf_op jit(solution)/shard_map/reduce_scatter | solution.py:223
  (248 shorter events, 267.5 us)
Async XLA Ops:
  7.2 65.5 %all-gather.15.cloned.1.call-start = ((), (), s32[]{:S(2)}) async-start(), calls=%async_computation.9 | async-start | bytes 2359296 | tf_op jit(solution)/shard_map/all_gather | solution.py:139
  9.2 76.6 %all-gather.11.cloned.1.call-start = ((), (), s32[]{:S(2)}) async-start(), calls=%async_computation.7 | async-start | bytes 2359296 | tf_op jit(solution)/shard_map/all_gather | solution.py:140
  11.1 100.8 %all-gather.13.cloned.1.call-start = ((), (), s32[]{:S(2)}) async-start(), calls=%async_computation.8 | async-start | bytes 2359296 | tf_op jit(solution)/shard_map/all_gather | solution.py:138
  11.9 172.5 %all-gather.17.cloned.1.call-start = ((), (), s32[]{:S(2)}) async-start(), calls=%async_computation.10 | async-start | bytes 2359296 | tf_op jit(solution)/shard_map/all_gather | solution.py:141
  12.7 251.0 %all-reduce.11.cloned.1.call-start = ((), (), s32[]{:S(2)}) async-start(), calls=%async_computation.11 | async-start | bytes 4194304 | tf_op jit(solution)/shard_map/psum | solution.py:191
  75.0 39.4 %collective-permute-start.6 = (bf16[256,512]{1,0:T(8,128)(2,1)S(1)}, bf16[256,512]{1,0:T(8,128)(2,1)S(1)}, u32[]{:S(2)}, u32[]{:S(2)}) collective-permute-start(bf16[256,512]{1,0:T(8,128)(2,1)S(1)} %convolution_convert_fusion.2), channel_id=1, source_target_pairs={{0,12},{4,16},{8,20},{12,24},{16,28},{1,13},{5,17},{9,21},{13,25},... | collective-permute-start | bytes 786440 | tf_op jit(solution)/shard_map/ppermute | solution.py:15
  78.5 37.2 %collective-permute-start.7 = (bf16[256,512]{1,0:T(8,128)(2,1)S(1)}, bf16[256,512]{1,0:T(8,128)(2,1)S(1)}, u32[]{:S(2)}, u32[]{:S(2)}) collective-permute-start(bf16[256,512]{1,0:T(8,128)(2,1)S(1)} %convolution_convert_fusion.2), channel_id=1, source_target_pairs={{0,8},{4,12},{8,16},{12,20},{16,24},{20,28},{1,9},{5,13},{9,17},{1... | collective-permute-start | bytes 786440 | tf_op jit(solution)/shard_map/ppermute | solution.py:15
  79.9 40.1 %collective-permute-start.8 = (bf16[256,512]{1,0:T(8,128)(2,1)S(1)}, bf16[256,512]{1,0:T(8,128)(2,1)S(1)}, u32[]{:S(2)}, u32[]{:S(2)}) collective-permute-start(bf16[256,512]{1,0:T(8,128)(2,1)S(1)} %convolution_convert_fusion.2), channel_id=1, source_target_pairs={{0,4},{4,8},{8,12},{12,16},{16,20},{20,24},{24,28},{1,5},{5,9},{9,... | collective-permute-start | bytes 786440 | tf_op jit(solution)/shard_map/ppermute | solution.py:15
  83.2 61.1 %collective-permute-start.9 = (bf16[256,512]{1,0:T(8,128)(2,1)S(1)}, bf16[256,512]{1,0:T(8,128)(2,1)S(1)}, u32[]{:S(2)}, u32[]{:S(2)}) collective-permute-start(bf16[256,512]{1,0:T(8,128)(2,1)S(1)} %convolution_convert_fusion.2), channel_id=1, source_target_pairs={{4,0},{8,4},{12,8},{16,12},{20,16},{24,20},{28,24},{5,1},{9,5},{13... | collective-permute-start | bytes 786440 | tf_op jit(solution)/shard_map/ppermute | solution.py:15
  84.5 61.5 %collective-permute-start.10 = (bf16[256,512]{1,0:T(8,128)(2,1)S(1)}, bf16[256,512]{1,0:T(8,128)(2,1)S(1)}, u32[]{:S(2)}, u32[]{:S(2)}) collective-permute-start(bf16[256,512]{1,0:T(8,128)(2,1)S(1)} %convolution_convert_fusion.2), channel_id=1, source_target_pairs={{8,0},{12,4},{16,8},{20,12},{24,16},{28,20},{9,1},{13,5},{17,9},{2... | collective-permute-start | bytes 786440 | tf_op jit(solution)/shard_map/ppermute | solution.py:15
  188.8 133.2 %all-gather.19.cloned.1.call-start = ((), (), s32[]{:S(2)}) async-start(), calls=%async_computation.12 | async-start | bytes 5898240 | tf_op jit(solution)/shard_map/all_gather | solution.py:186
  191.0 188.1 %all-gather.21.cloned.1.call-start = ((), (), s32[]{:S(2)}) async-start(), calls=%async_computation.13 | async-start | bytes 5898240 | tf_op jit(solution)/shard_map/all_gather | solution.py:187
  193.4 242.7 %all-gather.23.cloned.1.call-start = ((), (), s32[]{:S(2)}) async-start(), calls=%async_computation.14 | async-start | bytes 5898240 | tf_op jit(solution)/shard_map/all_gather | solution.py:188
  194.4 322.5 %all-reduce.15.cloned.1.call-start = ((), (), s32[]{:S(2)}) async-start(), calls=%async_computation.16 | async-start | bytes 4194304 | tf_op jit(solution)/shard_map/psum | solution.py:215
  448.9 124.1 %all-reduce.13.cloned.1.call-start = ((), (), s32[]{:S(2)}) async-start(), calls=%async_computation.15 | async-start | bytes 2097152 | tf_op jit(solution)/shard_map/psum | solution.py:200
  454.2 290.4 %all-reduce.17.cloned.1.call-start = ((), (), s32[]{:S(2)}) async-start(), calls=%async_computation.17 | async-start | bytes 4194304 | tf_op jit(solution)/shard_map/psum | solution.py:282
  618.5 31.8 %collective-permute-start.22 = (f32[256,512]{0,1:T(8,128)S(1)}, f32[256,512]{0,1:T(8,128)S(1)}, u32[]{:S(2)}, u32[]{:S(2)}) collective-permute-start(f32[256,512]{0,1:T(8,128)S(1)} %get-tuple-element.94), channel_id=1, source_target_pairs={{8,0},{12,4},{16,8},{20,12},{24,16},{28,20},{9,1},{13,5},{17,9},{2... | collective-permute-start | bytes 1572872 | tf_op jit(solution)/shard_map/ppermute | solution.py:15
  662.3 135.6 %reduce-scatter.8.cloned.1.call-start = ((), (), s32[]{:S(2)}) async-start(), calls=%async_computation.18 | async-start | bytes 4718592 | tf_op jit(solution)/shard_map/reduce_scatter | solution.py:286
  666.2 182.8 %reduce-scatter.14.cloned.1.call-start = ((), (), s32[]{:S(2)}) async-start(), calls=%async_computation.21 | async-start | bytes 4718592 | tf_op jit(solution)/shard_map/reduce_scatter | solution.py:289
  670.0 230.1 %reduce-scatter.10.cloned.1.call-start = ((), (), s32[]{:S(2)}) async-start(), calls=%async_computation.19 | async-start | bytes 4718592 | tf_op jit(solution)/shard_map/reduce_scatter | solution.py:287
  672.9 278.2 %reduce-scatter.12.cloned.1.call-start = ((), (), s32[]{:S(2)}) async-start(), calls=%async_computation.20 | async-start | bytes 4718592 | tf_op jit(solution)/shard_map/reduce_scatter | solution.py:288
  676.8 384.8 %reduce-scatter.16.cloned.1.call-start = ((), (), s32[]{:S(2)}) async-start(), calls=%async_computation.22 | async-start | bytes 11796480 | tf_op jit(solution)/shard_map/reduce_scatter | solution.py:221
  683.9 488.3 %reduce-scatter.18.cloned.1.call-start = ((), (), s32[]{:S(2)}) async-start(), calls=%async_computation.23 | async-start | bytes 11796480 | tf_op jit(solution)/shard_map/reduce_scatter | solution.py:222
  690.8 592.0 %reduce-scatter.20.cloned.1.call-start = ((), (), s32[]{:S(2)}) async-start(), calls=%async_computation.24 | async-start | bytes 11796480 | tf_op jit(solution)/shard_map/reduce_scatter | solution.py:223
  (51 other events, 874.4 us)
Sparse Core Ops, SparseCore 0:
  10.2 31.8 all-gather.14
  44.3 28.5 all-gather.10
  75.1 36.7 all-gather.12
  113.9 38.1 all-gather.16
  188.9 74.7 all-reduce.10
  265.9 56.0 all-gather.18
  324.3 54.8 all-gather.20
  380.8 55.2 all-gather.22
  449.0 67.8 all-reduce.14
  520.4 52.5 all-reduce.12
  662.5 82.0 all-reduce.16
  747.4 50.4 reduce-scatter.7
  800.9 48.0 reduce-scatter.13
  851.9 48.1 reduce-scatter.9
  902.9 48.1 reduce-scatter.11
  953.9 107.5 reduce-scatter.15
  1064.4 107.7 reduce-scatter.17
  1175.0 107.7 reduce-scatter.19
where the time goes:
time: 1300 us; the launch traced here: 1290 us
  waiting for transfers between devices  911 us (70%)
  matrix products  95.9 us (7%)
  local copies, waits for them, and re-layouts  86 us (7%)
  starting transfers between devices  79.2 us (6%)
  blocking collectives  68.4 us (5%)
  other arithmetic  32.5 us (2%)
  between operations  17.3 us (1%)
    reduce_scatter x1, waiting for transfers between devices, local(): lax.psum_scatter(d_down, 'fsdp', scatter_dimension=1, tiled=True)  111 us
    reduce_scatter x1, waiting for transfers between devices, local(): lax.psum_scatter(d_up_w, 'fsdp', scatter_dimension=0, tiled=True)  111 us
    reduce_scatter x1, waiting for transfers between devices, local(): lax.psum_scatter(d_gate_w, 'fsdp', scatter_dimension=0, tiled=True)  110 us
    ppermute x24, starting transfers between devices, shifted(): return lax.ppermute(block, axis, route)  78.2 us
    psum x1, waiting for transfers between devices, local(): lax.psum(contract_cols(d_gate_low, gate_full) + contract_cols(d_up_low, u...  62.4 us
    all_gather x1, waiting for transfers between devices, local(): lax.all_gather(w_gate.astype(low_type), 'fsdp', axis=0, tiled=True)  54.9 us
    psum x1, waiting for transfers between devices, local(): lax.psum(jnp.dot(hidden_act, down_full, preferred_element_type=jnp.float3...  53.9 us
    psum x1, waiting for transfers between devices, local(): lax.psum(jnp.dot(attended, out_full, preferred_element_type=jnp.float32),...  52.6 us
  transfers between devices with their start and end apart: 42, of which 22 were waited for; matrix products, arithmetic and copies ran while one was open for 13% of the time, Pallas kernels for 0%

commit v1 on v0

--- a/solution.py
+++ b/solution.py
@@ -7,6 +7,28 @@
 THRESHOLDS = (12, 16, 23, 32, 46, 64, 91)
 EPSILON = 1e-06
 MASKED = -1e30
+
+
+def laid_out(blocks, dim):
+    dims = list(blocks.shape[1:])
+    dims[dim] *= blocks.shape[0]
+    return jnp.moveaxis(blocks, 0, dim).reshape(dims)
+
+
+def collected_by_bits(value, axis):
+    size = lax.axis_size(axis)
+    parts = value[None]
+    for level in range(size.bit_length() - 1):
+        bit = 1 << level
+        received = lax.ppermute(parts, axis, [(i, i ^ bit) for i in range(size)])
+        both = jnp.stack([parts, received])
+        upper = lax.axis_index(axis) >> level & 1
+        parts = jnp.where(upper == 0, both, both[::-1]).reshape(-1, *value.shape)
+    return parts
+
+
+def collect(x, axis, dim):
+    return laid_out(collected_by_bits(x, axis), dim)
 
 
 def shifted(block, axis, distance):
@@ -185,7 +207,7 @@
         lax.all_gather(ffn_scale.astype(low_type), "fsdp", axis=0, tiled=True),
         lax.all_gather(w_gate.astype(low_type), "fsdp", axis=0, tiled=True),
         lax.all_gather(w_up.astype(low_type), "fsdp", axis=0, tiled=True),
-        lax.all_gather(w_down.astype(low_type), "fsdp", axis=1, tiled=True),
+        collect(w_down.astype(low_type), "fsdp", 1),
     )
     gain_two = gain_two.astype(jnp.float32)
     mixed_attn = lax.psum(jnp.dot(attended, out_full, preferred_element_type=jnp.float32), "mp")

time: 1300 us -> 1330 us (1.023)
  blocking collectives: 68.4 us -> 138 us
  waiting for transfers between devices: 911 us -> 851 us
    ppermute x0 -> x3, waiting for transfers between devices: none -> 142 us  [collected_by_bits(): received = lax.ppermute(parts, axis, [(i, i ^ bit) for i in range(size)])]
    all_gather x1, blocking collectives: 16 us -> 86 us  [local(): lax.all_gather(ffn_scale.astype(low_type), 'fsdp', axis=0, tiled=True)]
    all_gather x1, waiting for transfers between devices: 54.9 us -> 0.01 us  [local(): lax.all_gather(w_gate.astype(low_type), 'fsdp', axis=0, tiled=True)]
    psum x1, waiting for transfers between devices: 52.6 us -> 0.01 us  [local(): lax.psum(jnp.dot(attended, out_full, preferred_element_type=jnp.float32),...]
    all_gather x1, waiting for transfers between devices: 51.8 us -> 0.01 us  [local(): lax.all_gather(w_up.astype(low_type), 'fsdp', axis=0, tiled=True)]
    all_gather x1 -> x0, waiting for transfers between devices: 51.6 us -> none  [local(): lax.all_gather(w_down.astype(low_type), 'fsdp', axis=1, tiled=True)]
    unnamed x86 -> x94, local copies, waits for them, and re-layouts: 29.9 us -> 26.6 us
  transfers between devices with their start and end apart: 42 -> 44, of which waited for: 22 -> 21; matrix products, arithmetic and copies ran while one was open for 13% -> 14% of each run, Pallas kernels for 0% -> 0%
where the time goes in v1:
time: 1330 us; the launch traced here: 1320 us
  waiting for transfers between devices  851 us (64%)
  blocking collectives  138 us (10%)
  matrix products  94.1 us (7%)
  local copies, waits for them, and re-layouts  91.7 us (7%)
  starting transfers between devices  86.4 us (6%)
  other arithmetic  44 us (3%)
  between operations  17 us (1%)
    ppermute x3, waiting for transfers between devices, collected_by_bits(): received = lax.ppermute(parts, axis, [(i, i ^ bit) for i in range(size)])  142 us
    reduce_scatter x1, waiting for transfers between devices, local(): lax.psum_scatter(d_up_w, 'fsdp', scatter_dimension=0, tiled=True)  111 us
    reduce_scatter x1, waiting for transfers between devices, local(): lax.psum_scatter(d_down, 'fsdp', scatter_dimension=1, tiled=True)  111 us
    reduce_scatter x1, waiting for transfers between devices, local(): lax.psum_scatter(d_gate_w, 'fsdp', scatter_dimension=0, tiled=True)  110 us
    all_gather x1, blocking collectives, local(): lax.all_gather(ffn_scale.astype(low_type), 'fsdp', axis=0, tiled=True)  86 us
    ppermute x24, starting transfers between devices, shifted(): return lax.ppermute(block, axis, route)  78.1 us
    psum x1, waiting for transfers between devices, local(): lax.psum(contract_cols(d_gate_low, gate_full) + contract_cols(d_up_low, u...  71 us
    psum x1, waiting for transfers between devices, local(): lax.psum(jnp.dot(hidden_act, down_full, preferred_element_type=jnp.float3...  54.1 us
  transfers between devices with their start and end apart: 44, of which 21 were waited for; matrix products, arithmetic and copies ran while one was open for 14% of the time, Pallas kernels for 0%

profile of v1, /device:TPU:0, one launch (start us, length us, event | category | flops | bytes accessed | tf_op | source)
XLA Modules:
  0.0 1322.5 jit_solution(13872655754206626698)
XLA Ops:
  12.8 13.5 %all-gather = bf16[8,1,256]{2,1,0:T(2,128)(2,1)S(1)} all-gather(bf16[1,1,256]{2,1,0:T(2,128)(2,1)S(1)} %reshape.167), channel_id=1, replica_groups=mesh['fsdp'=8,'mp'=4] {'fsdp'}, dimensions={0}, use_global_device_ids=true | all-gather | bytes 4608 | tf_op jit(solution)/shard_map/all_gather | solution.py:159
  26.7 8.8 all-gather.1
  50.7 20.7 %reshape.152 = f32[8,256,1279]{2,1,0:T(8,128)} reshape(f32[2619392]{0:T(1024)} %reshape.178) | data formatting | bytes 20955136 | tf_op jit(solution)/shard_map/while/body/eval_jaxpr/reshape | solution.py:63
  88.2 23.7 %all-gather.12.cloned.1.call-done = bf16[2048,512]{1,0:T(8,128)(2,1)} async-done(((bf16[256,512]{1,0:T(8,128)(2,1)}), bf16[2048,512]{1,0:T(8,128)(2,1)}) %all-gather.12.cloned.1.call-update) | async-done | bytes 2097168 | tf_op jit(solution)/shard_map/all_gather | solution.py:160
  146.0 17.3 %collective-permute-done.4 = bf16[256,512]{1,0:T(8,128)(2,1)S(1)} collective-permute-done((bf16[256,512]{1,0:T(8,128)(2,1)S(1)}, bf16[256,512]{1,0:T(8,128)(2,1)S(1)}, u32[]{:S(2)}, u32[]{:S(2)}) %collective-permute-start.4) | collective-permute-done | bytes 262176 | tf_op jit(solution)/shard_map/ppermute | solution.py:37
  202.4 31.4 %collective-permute-done.13 = bf16[2,1280,256]{2,1,0:T(8,128)(2,1)} collective-permute-done((bf16[2,1280,256]{2,1,0:T(8,128)(2,1)}, bf16[2,1280,256]{2,1,0:T(8,128)(2,1)}, u32[]{:S(2)}, u32[]{:S(2)}) %collective-permute-start.13) | collective-permute-done | bytes 1310752 | tf_op jit(solution)/shard_map/ppermute | solution.py:23
  242.0 86.0 %all-gather.2 = bf16[8,1,256]{2,1,0:T(2,128)(2,1)S(1)} all-gather(bf16[1,1,256]{2,1,0:T(2,128)(2,1)S(1)} %reshape.171), channel_id=1, replica_groups=mesh['fsdp'=8,'mp'=4] {'fsdp'}, dimensions={0}, use_global_device_ids=true | all-gather | bytes 4608 | tf_op jit(solution)/shard_map/all_gather | solution.py:207
  333.2 109.4 %collective-permute-done.14 = bf16[4,1280,256]{1,2,0:T(8,128)(2,1)} collective-permute-done((bf16[4,1280,256]{1,2,0:T(8,128)(2,1)}, bf16[4,1280,256]{1,2,0:T(8,128)(2,1)}, u32[]{:S(2)}, u32[]{:S(2)}) %collective-permute-start.14) | collective-permute-done | bytes 2621472 | tf_op jit(solution)/shard_map/ppermute | solution.py:23
  478.3 71.0 %all-reduce.15.cloned.1.call-done = f32[256,2048]{1,0:T(8,128)} async-done(((f32[256,2048]{1,0:T(8,128)}), f32[256,2048]{1,0:T(8,128)}) %all-reduce.15.cloned.1.call-update) | async-done | bytes 2097168 | tf_op jit(solution)/shard_map/psum | solution.py:237
  551.5 54.1 %all-reduce.13.cloned.1.call-done = bf16[256,2048]{1,0:T(8,128)(2,1)} async-done(((bf16[256,2048]{1,0:T(8,128)(2,1)}), bf16[256,2048]{1,0:T(8,128)(2,1)}) %all-reduce.13.cloned.1.call-update) | async-done | bytes 1048592 | tf_op jit(solution)/shard_map/psum | solution.py:222
  655.0 14.0 %collective-permute-start.23 = (f32[256,512]{0,1:T(8,128)S(1)}, f32[256,512]{0,1:T(8,128)S(1)}, u32[]{:S(2)}, u32[]{:S(2)}) collective-permute-start(f32[256,512]{0,1:T(8,128)S(1)} %get-tuple-element.96), channel_id=1, source_target_pairs={{0,12},{4,16},{8,20},{12,24},{16,28},{1,13},{5,17},{9,21},{13,25},... | collective-permute-start | bytes 1572872 | tf_op jit(solution)/shard_map/ppermute | solution.py:37
  672.7 9.0 collective-permute-start.21
  682.9 8.8 collective-permute-done.22
  738.0 11.6 reshape.180
  749.6 10.4 reshape.162
  766.0 11.1 all-reduce.17.cloned.1.call-done
  779.3 29.8 %all-reduce.5 = (f32[2048]{0:T(1024)S(1)}, f32[32,8]{1,0:T(8,128)S(1)}, f32[2048]{0:T(1024)S(1)}) all-reduce(f32[2048]{0:T(1024)S(1)} %get-tuple-element.67, f32[32,8]{1,0:T(8,128)S(1)} %fusion.38, f32[2048]{0:T(1024)S(1)} %get-tuple-element.65), channel_id=2, replica_groups=mesh['fsdp'=8,'mp'=4] {'fsdp'}, use_global_device_ids=true, to_apply=%region_12.13.clone | all-reduce | flops 4352 | bytes 34816
  814.2 16.4 %reduce-scatter.8.cloned.1.call-done = f32[256,512]{1,0:T(8,128)} async-done(((f32[2048,512]{1,0:T(8,128)}), f32[256,512]{1,0:T(8,128)}) %reduce-scatter.8.cloned.1.call-update) | async-done | bytes 524304 | tf_op jit(solution)/shard_map/reduce_scatter | solution.py:308
  830.6 50.9 %reduce-scatter.14.cloned.1.call-done = f32[512,256]{1,0:T(8,128)} async-done(((f32[512,2048]{1,0:T(8,128)}), f32[512,256]{1,0:T(8,128)}) %reduce-scatter.14.cloned.1.call-update) | async-done | bytes 524304 | tf_op jit(solution)/shard_map/reduce_scatter | solution.py:311
  881.6 51.2 %reduce-scatter.10.cloned.1.call-done = f32[256,512]{1,0:T(8,128)} async-done(((f32[2048,512]{1,0:T(8,128)}), f32[256,512]{1,0:T(8,128)}) %reduce-scatter.10.cloned.1.call-update) | async-done | bytes 524304 | tf_op jit(solution)/shard_map/reduce_scatter | solution.py:309
  932.7 51.0 %reduce-scatter.12.cloned.1.call-done = f32[256,512]{1,0:T(8,128)} async-done(((f32[2048,512]{1,0:T(8,128)}), f32[256,512]{1,0:T(8,128)}) %reduce-scatter.12.cloned.1.call-update) | async-done | bytes 524304 | tf_op jit(solution)/shard_map/reduce_scatter | solution.py:310
  983.8 110.4 %reduce-scatter.16.cloned.1.call-done = f32[256,1280]{1,0:T(8,128)} async-done(((f32[2048,1280]{1,0:T(8,128)}), f32[256,1280]{1,0:T(8,128)}) %reduce-scatter.16.cloned.1.call-update) | async-done | bytes 1310736 | tf_op jit(solution)/shard_map/reduce_scatter | solution.py:243
  1094.2 110.6 %reduce-scatter.18.cloned.1.call-done = f32[256,1280]{1,0:T(8,128)} async-done(((f32[2048,1280]{1,0:T(8,128)}), f32[256,1280]{1,0:T(8,128)}) %reduce-scatter.18.cloned.1.call-update) | async-done | bytes 1310736 | tf_op jit(solution)/shard_map/reduce_scatter | solution.py:244
  1204.8 110.6 %reduce-scatter.20.cloned.1.call-done = f32[1280,256]{1,0:T(8,128)} async-done(((f32[1280,2048]{1,0:T(8,128)}), f32[1280,256]{1,0:T(8,128)}) %reduce-scatter.20.cloned.1.call-update) | async-done | bytes 1310736 | tf_op jit(solution)/shard_map/reduce_scatter | solution.py:245
  (269 shorter events, 273.4 us)
Async XLA Ops:
  7.2 65.4 %all-gather.14.cloned.1.call-start = ((), (), s32[]{:S(2)}) async-start(), calls=%async_computation.9 | async-start | bytes 2359296 | tf_op jit(solution)/shard_map/all_gather | solution.py:161
  9.2 76.6 %all-gather.10.cloned.1.call-start = ((), (), s32[]{:S(2)}) async-start(), calls=%async_computation.7 | async-start | bytes 2359296 | tf_op jit(solution)/shard_map/all_gather | solution.py:162
  11.1 100.8 %all-gather.12.cloned.1.call-start = ((), (), s32[]{:S(2)}) async-start(), calls=%async_computation.8 | async-start | bytes 2359296 | tf_op jit(solution)/shard_map/all_gather | solution.py:160
  11.9 172.5 %all-gather.16.cloned.1.call-start = ((), (), s32[]{:S(2)}) async-start(), calls=%async_computation.10 | async-start | bytes 2359296 | tf_op jit(solution)/shard_map/all_gather | solution.py:163
  12.7 436.1 %all-reduce.11.cloned.1.call-start = ((), (), s32[]{:S(2)}) async-start(), calls=%async_computation.11 | async-start | bytes 4194304 | tf_op jit(solution)/shard_map/psum | solution.py:213
  75.0 39.4 %collective-permute-start.6 = (bf16[256,512]{1,0:T(8,128)(2,1)S(1)}, bf16[256,512]{1,0:T(8,128)(2,1)S(1)}, u32[]{:S(2)}, u32[]{:S(2)}) collective-permute-start(bf16[256,512]{1,0:T(8,128)(2,1)S(1)} %convolution_convert_fusion.2), channel_id=1, source_target_pairs={{0,12},{4,16},{8,20},{12,24},{16,28},{1,13},{5,17},{9,21},{13,25},... | collective-permute-start | bytes 786440 | tf_op jit(solution)/shard_map/ppermute | solution.py:37
  78.5 37.2 %collective-permute-start.7 = (bf16[256,512]{1,0:T(8,128)(2,1)S(1)}, bf16[256,512]{1,0:T(8,128)(2,1)S(1)}, u32[]{:S(2)}, u32[]{:S(2)}) collective-permute-start(bf16[256,512]{1,0:T(8,128)(2,1)S(1)} %convolution_convert_fusion.2), channel_id=1, source_target_pairs={{0,8},{4,12},{8,16},{12,20},{16,24},{20,28},{1,9},{5,13},{9,17},{1... | collective-permute-start | bytes 786440 | tf_op jit(solution)/shard_map/ppermute | solution.py:37
  79.9 40.2 %collective-permute-start.8 = (bf16[256,512]{1,0:T(8,128)(2,1)S(1)}, bf16[256,512]{1,0:T(8,128)(2,1)S(1)}, u32[]{:S(2)}, u32[]{:S(2)}) collective-permute-start(bf16[256,512]{1,0:T(8,128)(2,1)S(1)} %convolution_convert_fusion.2), channel_id=1, source_target_pairs={{0,4},{4,8},{8,12},{12,16},{16,20},{20,24},{24,28},{1,5},{5,9},{9,... | collective-permute-start | bytes 786440 | tf_op jit(solution)/shard_map/ppermute | solution.py:37
  83.2 61.2 %collective-permute-start.9 = (bf16[256,512]{1,0:T(8,128)(2,1)S(1)}, bf16[256,512]{1,0:T(8,128)(2,1)S(1)}, u32[]{:S(2)}, u32[]{:S(2)}) collective-permute-start(bf16[256,512]{1,0:T(8,128)(2,1)S(1)} %convolution_convert_fusion.2), channel_id=1, source_target_pairs={{4,0},{8,4},{12,8},{16,12},{20,16},{24,20},{28,24},{5,1},{9,5},{13... | collective-permute-start | bytes 786440 | tf_op jit(solution)/shard_map/ppermute | solution.py:37
  84.5 61.4 %collective-permute-start.10 = (bf16[256,512]{1,0:T(8,128)(2,1)S(1)}, bf16[256,512]{1,0:T(8,128)(2,1)S(1)}, u32[]{:S(2)}, u32[]{:S(2)}) collective-permute-start(bf16[256,512]{1,0:T(8,128)(2,1)S(1)} %convolution_convert_fusion.2), channel_id=1, source_target_pairs={{8,0},{12,4},{16,8},{20,12},{24,16},{28,20},{9,1},{13,5},{17,9},{2... | collective-permute-start | bytes 786440 | tf_op jit(solution)/shard_map/ppermute | solution.py:37
  188.2 264.0 %all-gather.18.cloned.1.call-start = ((), (), s32[]{:S(2)}) async-start(), calls=%async_computation.12 | async-start | bytes 5898240 | tf_op jit(solution)/shard_map/all_gather | solution.py:208
  190.6 267.0 %all-gather.20.cloned.1.call-start = ((), (), s32[]{:S(2)}) async-start(), calls=%async_computation.13 | async-start | bytes 5898240 | tf_op jit(solution)/shard_map/all_gather | solution.py:209
  200.0 349.3 %all-reduce.15.cloned.1.call-start = ((), (), s32[]{:S(2)}) async-start(), calls=%async_computation.15 | async-start | bytes 4194304 | tf_op jit(solution)/shard_map/psum | solution.py:237
  242.0 200.6 %collective-permute-start.14 = (bf16[4,1280,256]{1,2,0:T(8,128)(2,1)}, bf16[4,1280,256]{1,2,0:T(8,128)(2,1)}, u32[]{:S(2)}, u32[]{:S(2)}) collective-permute-start(bf16[4,1280,256]{1,2,0:T(8,128)(2,1)} %copy.38), channel_id=1, source_target_pairs={{0,16},{4,20},{8,24},{12,28},{16,0},{20,4},{24,8},{28,12},{1,17},{... | collective-permute-start | bytes 7864328 | tf_op jit(solution)/shard_map/ppermute | solution.py:23
  472.7 132.8 %all-reduce.13.cloned.1.call-start = ((), (), s32[]{:S(2)}) async-start(), calls=%async_computation.14 | async-start | bytes 2097152 | tf_op jit(solution)/shard_map/psum | solution.py:222
  478.0 299.1 %all-reduce.17.cloned.1.call-start = ((), (), s32[]{:S(2)}) async-start(), calls=%async_computation.16 | async-start | bytes 4194304 | tf_op jit(solution)/shard_map/psum | solution.py:304
  651.0 31.8 %collective-permute-start.25 = (f32[256,512]{0,1:T(8,128)S(1)}, f32[256,512]{0,1:T(8,128)S(1)}, u32[]{:S(2)}, u32[]{:S(2)}) collective-permute-start(f32[256,512]{0,1:T(8,128)S(1)} %get-tuple-element.94), channel_id=1, source_target_pairs={{8,0},{12,4},{16,8},{20,12},{24,16},{28,20},{9,1},{13,5},{17,9},{2... | collective-permute-start | bytes 1572872 | tf_op jit(solution)/shard_map/ppermute | solution.py:37
  694.9 135.8 %reduce-scatter.8.cloned.1.call-start = ((), (), s32[]{:S(2)}) async-start(), calls=%async_computation.17 | async-start | bytes 4718592 | tf_op jit(solution)/shard_map/reduce_scatter | solution.py:308
  698.8 182.8 %reduce-scatter.14.cloned.1.call-start = ((), (), s32[]{:S(2)}) async-start(), calls=%async_computation.20 | async-start | bytes 4718592 | tf_op jit(solution)/shard_map/reduce_scatter | solution.py:311
  702.5 230.2 %reduce-scatter.10.cloned.1.call-start = ((), (), s32[]{:S(2)}) async-start(), calls=%async_computation.18 | async-start | bytes 4718592 | tf_op jit(solution)/shard_map/reduce_scatter | solution.py:309
  705.4 278.4 %reduce-scatter.12.cloned.1.call-start = ((), (), s32[]{:S(2)}) async-start(), calls=%async_computation.19 | async-start | bytes 4718592 | tf_op jit(solution)/shard_map/reduce_scatter | solution.py:310
  709.3 384.9 %reduce-scatter.16.cloned.1.call-start = ((), (), s32[]{:S(2)}) async-start(), calls=%async_computation.21 | async-start | bytes 11796480 | tf_op jit(solution)/shard_map/reduce_scatter | solution.py:243
  716.4 488.5 %reduce-scatter.18.cloned.1.call-start = ((), (), s32[]{:S(2)}) async-start(), calls=%async_computation.22 | async-start | bytes 11796480 | tf_op jit(solution)/shard_map/reduce_scatter | solution.py:244
  723.3 592.2 %reduce-scatter.20.cloned.1.call-start = ((), (), s32[]{:S(2)}) async-start(), calls=%async_computation.23 | async-start | bytes 11796480 | tf_op jit(solution)/shard_map/reduce_scatter | solution.py:245
  (57 other events, 811.4 us)
Sparse Core Ops, SparseCore 0:
  10.2 31.8 all-gather.13
  44.3 28.5 all-gather.9
  75.1 36.7 all-gather.11
  113.9 38.1 all-gather.15
  188.3 74.7 all-reduce.10
  265.3 101.0 all-gather.17
  368.2 75.8 all-gather.19
  472.9 76.3 all-reduce.14
  552.9 52.5 all-reduce.12
  695.0 82.0 all-reduce.16
  780.1 50.5 reduce-scatter.7
  833.5 48.0 reduce-scatter.13
  884.6 48.1 reduce-scatter.9
  935.6 48.1 reduce-scatter.11
  986.6 107.5 reduce-scatter.15
  1097.0 107.7 reduce-scatter.17
  1207.7 107.7 reduce-scatter.19
